TPU v7x, 32 devices: a whole 2x2x4 slice. The times are simulated.
32 devices in a mesh: sy: 4 (over z), sx: 4 (over y, core), tp: 2 (over x).
Axes of the slice: x: 2, y: 2, z: 4, core: 2. Of those that a mesh axis runs over, the one named last changes fastest.
Arguments:
- features: bfloat16 [96, 64, 1408], P('sy', 'sx', 'tp'), may hold values from -6 to 6
- depth_kernel: float32 [7, 7, 1408], P(None, None, 'tp'), may hold values from -0.875 to 0.875
- depth_bias: float32 [1408], P('tp'), may hold values from -1 to 1
- norm_gain: float32 [1408], replicated, may hold values from 0.1 to 1.9
- norm_bias: float32 [1408], replicated, may hold values from -3 to 3
- up_weight: bfloat16 [1408, 5632], P(None, 'tp'), may hold values from -0.15625 to 0.15625
- up_bias: float32 [5632], P('tp'), may hold values from -3 to 3
- response_gain: float32 [5632], P('tp'), may hold values from -4 to 4
- response_shift: float32 [5632], P('tp'), may hold values from -3 to 3
- down_weight: bfloat16 [5632, 1408], P('tp', ('sy', 'sx')), may hold values from -0.078125 to 0.078125
- down_bias: float32 [1408], P('tp'), may hold values from -3 to 3
- tissue: int32 [12, 8], P('sy', 'sx'), may hold values from 0 to 1, as said below
- cotangent: bfloat16 [96, 64, 1408], P('sy', 'sx', 'tp'), may hold values from -6 to 6
Outputs:
- block_out: bfloat16 [96, 64, 1408], P('sy', 'sx', 'tp')
- feature_grad: bfloat16 [96, 64, 1408], P('sy', 'sx', 'tp')
Inputs may be any that keep to these rules, and one draw needn't show every extreme that they name: Each device's block of 3 x 2 tiles holds 1 to 4 tissue tiles; some device's block holds exactly 4.
All inputs are finite; a program needn't handle non-finite values.
Results may differ from a plain program's by a relative error of at most 0.0049.
The roundings to bfloat16 on the way count: a program that leaves them out, or rounds other values in their place, can miss the bound.
Values may be sent and summed in bfloat16 or wider, within the bound.
A program may use at most 128 MiB of HBM per device.

v0:
```python
import jax
import jax.numpy as jnp
from jax import lax
from jax.sharding import PartitionSpec as P

KERNEL = 7
TILE = 8
root_half = 0.7071067811865476
root_two_pi_inv = 0.3989422804014327


def extended(block, sides, width):
    for axis, dim in sides:
        count = lax.axis_size(axis)
        forward = [(i, i + 1) for i in range(count - 1)]
        backward = [(target, source) for source, target in forward]
        low = lax.ppermute(
            lax.slice_in_dim(block, block.shape[dim] - width, None, axis=dim), axis, forward
        )
        high = lax.ppermute(lax.slice_in_dim(block, 0, width, axis=dim), axis, backward)
        block = jnp.concatenate([low, block, high], axis=dim)
    return block


def gelu_value(values):
    return 0.5 * values * (1.0 + jax.scipy.special.erf(values * root_half))


def gelu_slope(values):
    return (
        0.5 * (1.0 + jax.scipy.special.erf(values * root_half))
        + values * jnp.exp(-0.5 * values * values) * root_two_pi_inv
    )


def depthwise(padded, kernel, rows_out, cols_out, flipped):
    summed = jnp.zeros((rows_out, cols_out, kernel.shape[2]), jnp.float32)
    last_tap = KERNEL - 1
    for row_tap in range(KERNEL):
        for col_tap in range(KERNEL):
            row_start = last_tap - row_tap if flipped else row_tap
            col_start = last_tap - col_tap if flipped else col_tap
            window = padded[row_start : row_start + rows_out, col_start : col_start + cols_out]
            summed = summed + window.astype(jnp.float32) * kernel[row_tap, col_tap]
    return summed


def extend(image):
    return extended(image, (("sy", 0), ("sx", 1)), KERNEL // 2)


def all_channels(rows_array):
    return lax.all_gather(rows_array, "tp", axis=1, tiled=True)


def global_vector(local_part):
    hidden_local = local_part.shape[0]
    placed = lax.dynamic_update_slice(
        jnp.zeros((hidden_local * lax.axis_size("tp"),), jnp.float32),
        local_part,
        (lax.axis_index("tp") * hidden_local,),
    )
    return lax.psum(placed, ("sy", "sx", "tp"))


def shards(
    features,
    depth_kernel,
    depth_bias,
    norm_gain,
    norm_bias,
    up_weight,
    up_bias,
    response_gain,
    response_shift,
    down_weight,
    down_bias,
    tissue,
    cotangent,
):
    image_rows, image_cols, local_channels = features.shape
    hidden_local = up_weight.shape[1]
    channel_start = lax.axis_index("tp") * local_channels
    contract_last = (((1,), (1,)), ((), ()))
    pixel_mask = jnp.repeat(jnp.repeat(tissue, TILE, axis=0), TILE, axis=1).astype(jnp.float32)
    mask_rows = pixel_mask.reshape(-1)

    def select(image):
        return image.reshape(image_rows * image_cols, image.shape[2])

    def restore(rows_array):
        return rows_array.reshape(image_rows, image_cols, rows_array.shape[1])

    convolved = (
        depthwise(extend(features), depth_kernel, image_rows, image_cols, False) + depth_bias
    ).astype(jnp.bfloat16)
    gathered = all_channels(select(convolved)).astype(jnp.float32)
    centre = jnp.mean(gathered, axis=1, keepdims=True)
    spread = jnp.mean(jnp.square(gathered - centre), axis=1, keepdims=True)
    inv_scale = lax.rsqrt(spread + 1e-06)
    standard = (gathered - centre) * inv_scale
    normed = (standard * norm_gain + norm_bias).astype(jnp.bfloat16)
    preact = jnp.dot(normed, up_weight, preferred_element_type=jnp.float32) + up_bias
    hidden = gelu_value(preact).astype(jnp.bfloat16)
    hidden_wide = hidden.astype(jnp.float32)
    squares = global_vector(jnp.sum(mask_rows[:, None] * hidden_wide * hidden_wide, axis=0))
    all_norms = jnp.sqrt(squares)
    norm_level = jnp.mean(all_norms) + 1e-06
    unit_start = lax.axis_index("tp") * hidden_local
    column_norms = lax.dynamic_slice_in_dim(all_norms, unit_start, hidden_local)
    norm_ratio = column_norms / norm_level
    response = (response_gain * hidden_wide * norm_ratio + response_shift + hidden_wide).astype(
        jnp.bfloat16
    )
    down_whole = lax.all_gather(down_weight, ("sy", "sx"), axis=1, tiled=True)
    partial_out = jnp.dot(response, down_whole, preferred_element_type=jnp.float32)
    branch = lax.psum_scatter(partial_out, "tp", scatter_dimension=1, tiled=True)
    branch_image = restore(branch + down_bias)
    block_out = (features.astype(jnp.float32) + pixel_mask[:, :, None] * branch_image).astype(
        jnp.bfloat16
    )
    masked_cot = (select(cotangent).astype(jnp.float32) * mask_rows[:, None]).astype(jnp.bfloat16)
    cot_wide = all_channels(masked_cot)
    back_hidden = lax.dot_general(
        cot_wide, down_whole, contract_last, preferred_element_type=jnp.float32
    )
    ratio_grad = global_vector(response_gain * jnp.sum(back_hidden * hidden_wide, axis=0))
    ratio_local = lax.dynamic_slice_in_dim(ratio_grad, unit_start, hidden_local)
    norms_grad = ratio_local / norm_level - jnp.sum(ratio_grad * all_norms) / (
        all_norms.shape[0] * norm_level * norm_level
    )
    hidden_grad = (
        back_hidden * (response_gain * norm_ratio + 1.0)
        + norms_grad * mask_rows[:, None] * hidden_wide / column_norms
    )
    preact_grad = (hidden_grad * gelu_slope(preact)).astype(jnp.bfloat16)
    grad_terms = lax.dot_general(
        preact_grad, up_weight, contract_last, preferred_element_type=jnp.float32
    )
    normed_grad = lax.psum(grad_terms, "tp")
    scaled = normed_grad * norm_gain
    convolved_grad = inv_scale * (
        scaled
        - jnp.mean(scaled, axis=1, keepdims=True)
        - standard * jnp.mean(scaled * standard, axis=1, keepdims=True)
    )
    convolved_grad = convolved_grad.astype(jnp.bfloat16)
    local_grad = lax.dynamic_slice_in_dim(convolved_grad, channel_start, local_channels, 1)
    grad_image = restore(local_grad)
    feature_grad = (
        cotangent.astype(jnp.float32)
        + depthwise(extend(grad_image), depth_kernel, image_rows, image_cols, True)
    ).astype(jnp.bfloat16)
    return (block_out, feature_grad)


def solution(mesh):
    placed = (
        P("sy", "sx", "tp"),
        P(None, None, "tp"),
        P("tp"),
        P(),
        P(),
        P(None, "tp"),
        P("tp"),
        P("tp"),
        P("tp"),
        P("tp", ("sy", "sx")),
        P("tp"),
        P("sy", "sx"),
        P("sy", "sx", "tp"),
    )
    return jax.shard_map(
        shards,
        mesh=mesh,
        in_specs=placed,
        out_specs=(P("sy", "sx", "tp"), P("sy", "sx", "tp")),
        check_vma=False,
    )
```

profile of v0, /device:TPU:0, one launch (start us, length us, event | category | flops | bytes accessed | tf_op | source)
XLA Modules:
  0.0 338.2 jit_solution(16324802515780690744)
XLA Ops:
  7.2 0.0 all-gather.4.cloned.1.call-start
  7.2 0.9 fusion.105
  8.1 4.9 %collective-permute-start = (bf16[3,16,704]{2,1,0:T(8,128)(2,1)S(1)}, bf16[3,16,704]{2,1,0:T(8,128)(2,1)S(1)}, u32[]{:S(2)}, u32[]{:S(2)}) collective-permute-start(bf16[3,16,704]{2,1,0:T(8,128)(2,1)S(1)} %get-tuple-element.77), channel_id=1, source_target_pairs={{0,8},{8,16},{16,24},{1,9},{9,17},{17,25},{2,10},{10,18},{18,26},{... | collective-permute-start | bytes 202760 | tf_op jit(solution)/shard_map/ppermute | solution.py:17
  13.1 1.3 collective-permute-start.1
  14.4 1.4 slice_reduce_fusion.48
  15.8 1.1 slice_reduce_fusion.46
  16.9 1.2 constant_dynamic-update-slice_fusion.3
  18.2 1.2 collective-permute-done.1
  19.3 0.1 fusion.103
  19.5 1.3 collective-permute-start.2
  20.8 1.3 collective-permute-start.3
  22.1 1.4 slice_reduce_fusion.47
  23.5 2.4 collective-permute-done.3
  25.9 14.1 %add_convert_fusion.2 = bf16[24,16,704]{2,1,0:T(8,128)(2,1)S(1)} fusion(bf16[24,16,704]{2,1,0:T(8,128)(2,1)S(1)} %copy-done, bf16[30,16,704]{2,1,0:T(8,128)(2,1)S(1)} %get-tuple-element.81, bf16[30,3,704]{2,1,0:T(4,128)(2,1)S(1)} %collective-permute-done.3, bf16[30,3,704]{2,1,0:T(4,128)(2,1)S(1)} %collective-permute-done.2, ...), kind=kLoop, calls=%fused_computation.149 | loop fusion | flops 74072064 | bytes 5395456 | tf_op jit(solution)/shard_map/convert_element_type | solution.py:96
  40.0 1.0 copy.21
  41.0 0.0 all-gather.4.cloned.1.call-update
  41.0 0.0 all-gather.8.cloned.1.call-start
  41.1 0.1 broadcast_in_dim.4
  41.2 0.1 convert_element_type.364
  41.3 0.1 copy.26
  41.4 0.1 broadcast_in_dim.5.clone
  41.4 0.1 convert_element_type.419
  41.6 0.2 copy.25
  41.8 0.9 multiply_convert_fusion.1
  42.7 0.0 all-gather.8.cloned.1.call-update
  42.7 0.0 all-gather.6.cloned.1.call-start
  42.7 0.7 all-gather.6.cloned.1.call-update
  43.4 0.0 all-reduce.3.cloned.1.call-start
  43.5 23.3 %all-gather.4.cloned.1.call-done = bf16[384,1408]{0,1:T(8,128)(2,1)} async-done(((bf16[384,704]{0,1:T(8,128)(2,1)}), bf16[384,1408]{0,1:T(8,128)(2,1)}) %all-gather.4.cloned.1.call-update) | async-done | bytes 1081360 | tf_op jit(solution)/shard_map/all_gather | solution.py:53
  66.7 1.7 copy.22
  68.5 0.2 convert_reduce_fusion
  68.7 0.4 fusion.15
  69.2 0.0 copy-done.7
  69.2 8.6 %convolution_add_fusion = f32[384,2816]{1,0:T(8,128)} fusion(bf16[1408,2816]{1,0:T(8,128)(2,1)} %param.18, f32[2816]{0:T(1024)S(1)} %copy-done.7, f32[1408]{0:T(1024)S(1)} %copy-done.9, f32[1408]{0:T(1024)S(1)} %copy-done.3, bf16[384,1408]{1,0:T(8,128)(2,1)S(1)} %copy.22, f32[384]{0:T(512)S(1)} %add_rsqrt_fusion, f32[384]{0:T(512)S(1)} %broadcast_multiply_fusion.3), kind=kOutput, calls=%fused_computation.62 | convolution fusion | flops 3049390080 | bytes 13362176 | tf_op jit(solution)/shard_map/dot_general | solution.py:103
  77.8 12.8 %all-gather.8.cloned.1.call-done = bf16[384,1408]{0,1:T(8,128)(2,1)} async-done(((bf16[384,704]{0,1:T(8,128)(2,1)}), bf16[384,1408]{0,1:T(8,128)(2,1)}) %all-gather.8.cloned.1.call-update) | async-done | bytes 1081360 | tf_op jit(solution)/shard_map/all_gather | solution.py:53
  90.6 74.2 %all-gather.6.cloned.1.call-done = bf16[2816,1408]{0,1:T(8,128)(2,1)} async-done(((bf16[2816,88]{0,1:T(8,128)(2,1)}), bf16[2816,1408]{0,1:T(8,128)(2,1)}) %all-gather.6.cloned.1.call-update) | async-done | bytes 7929872 | tf_op jit(solution)/shard_map/all_gather | solution.py:115
  164.8 9.9 %fusion.10 = (f32[2816]{0:T(1024)S(1)}, f32[2816]{0:T(1024)S(1)}, bf16[384,2816]{1,0:T(8,128)(2,1)}, f32[384,2816]{1,0:T(8,128)}) fusion(f32[384]{0:T(512)S(1)} %convert_element_type.419, f32[384,2816]{1,0:T(8,128)} %convolution_add_fusion, bf16[384,1408]{0,1:T(8,128)(2,1)} %all-gather.8.cloned.1.call-done, bf16[2816,1408]{0,1:T(8,128)(2,1)} %all-gather.6.cloned.1.call-done), kind=kOutput, calls=%fused_computation.57 | convolution fusion | flops 3056953856 | bytes 19848704 | tf_op jit(solution)/shard_map/dot_general | solution.py:124
  174.7 0.3 dynamic_update_slice.6
  175.0 0.1 multiply_dynamic-update-slice_fusion
  175.2 39.6 %all-reduce = (f32[5632]{0:T(1024)S(1)}, f32[5632]{0:T(1024)S(1)}) all-reduce(f32[5632]{0:T(1024)S(1)} %dynamic_update_slice.6, f32[5632]{0:T(1024)S(1)} %multiply_dynamic-update-slice_fusion), channel_id=1, replica_groups=mesh['sy'=4,'sx'=4,'tp'=2] {'sy','sx','tp'}, use_global_device_ids=true, to_apply=%region_3.0 | all-reduce | flops 11264 | bytes 90112 | tf_op jit(solution)/shard_map/psum | solution.py:63
  214.7 0.6 multiply_reduce_fusion.1
  216.6 0.1 multiply_add_fusion
  216.7 12.4 %fusion.21 = f32[384,1408]{1,0:T(8,128)} fusion(bf16[1408,2816]{1,0:T(8,128)(2,1)} %param.18, f32[384,2816]{1,0:T(8,128)} %convolution_add_fusion, bf16[384,2816]{1,0:T(8,128)(2,1)} %get-tuple-element.63, f32[384,2816]{1,0:T(8,128)} %get-tuple-element.83, f32[2816]{0:T(1024)S(1)} %get-tuple-element.62, f32[2816]{0:T(1024)S(1)} %get-tuple-element.84, ...), kind=kOutput, calls=%fused_computation.74 | convolution fusion | flops 3062366208 | bytes 20941312 | tf_op jit(solution)/shard_map/dot_general | solution.py:137
  229.1 0.0 reduce-scatter.2.cloned.1.call-start
  229.2 0.6 copy-done.8
  229.8 9.6 %fusion.16 = f32[384,1408]{0,1:T(8,128)} fusion(bf16[2816,1408]{0,1:T(8,128)(2,1)} %all-gather.6.cloned.1.call-done, bf16[384,2816]{1,0:T(8,128)(2,1)} %get-tuple-element.63, f32[2816]{0:T(1024)S(1)} %copy-done.8, f32[2816]{0:T(1024)S(1)} %get-tuple-element.61, f32[2816]{0:T(1024)S(1)} %copy-done.2), kind=kOutput, calls=%fused_computation.68 | convolution fusion | flops 3051552768 | bytes 12289024 | tf_op jit(solution)/shard_map/dot_general | solution.py:116
  239.4 54.7 %all-reduce.3.cloned.1.call-done = f32[384,1408]{1,0:T(8,128)} async-done(((f32[384,1408]{1,0:T(8,128)}), f32[384,1408]{1,0:T(8,128)}) %all-reduce.3.cloned.1.call-update) | async-done | bytes 2162704 | tf_op jit(solution)/shard_map/psum | solution.py:140
  294.1 2.3 fusion.102
  296.4 1.0 fusion.51
  297.4 3.4 %collective-permute-start.4 = (bf16[3,16,704]{2,1,0:T(8,128)(2,1)S(1)}, bf16[3,16,704]{2,1,0:T(8,128)(2,1)S(1)}, u32[]{:S(2)}, u32[]{:S(2)}) collective-permute-start(bf16[3,16,704]{2,1,0:T(8,128)(2,1)S(1)} %bitcast.23), channel_id=1, source_target_pairs={{0,8},{8,16},{16,24},{1,9},{9,17},{17,25},{2,10},{10,18},{18,26},{... | collective-permute-start | bytes 202760 | tf_op jit(solution)/shard_map/ppermute | solution.py:17
  300.8 1.3 collective-permute-start.5
  302.1 0.7 collective-permute-done.4
  302.7 4.3 %collective-permute-done.5 = bf16[3,16,704]{2,1,0:T(8,128)(2,1)S(1)} collective-permute-done((bf16[3,16,704]{2,1,0:T(8,128)(2,1)S(1)}, bf16[3,16,704]{2,1,0:T(8,128)(2,1)S(1)}, u32[]{:S(2)}, u32[]{:S(2)}) %collective-permute-start.5) | collective-permute-done | bytes 67616 | tf_op jit(solution)/shard_map/ppermute | solution.py:20
  307.0 0.2 pad_maximum_fusion.7
  307.2 1.3 collective-permute-start.6
  308.5 3.3 collective-permute-start.7
  311.8 0.1 copy.20
  311.8 0.7 collective-permute-done.7
  312.6 0.6 pad_maximum_fusion
  313.1 10.3 %add_convert_fusion.1 = bf16[24,16,704]{2,1,0:T(8,128)(2,1)} fusion(bf16[24,16,704]{2,1,0:T(8,128)(2,1)S(1)} %bitcast.18, bf16[3,16,704]{2,1,0:T(8,128)(2,1)S(1)} %collective-permute-done.4, bf16[3,16,704]{2,1,0:T(8,128)(2,1)S(1)} %collective-permute-done.5, bf16[30,19,704]{2,1,0:T(8,128)(2,1)S(1)} %get-tuple-element.66, ...), kind=kLoop, calls=%fused_computation.148 | loop fusion | flops 41902080 | bytes 24603392 | tf_op jit(solution)/shard_map/convert_element_type | solution.py:153
  323.5 5.4 %reduce-scatter.2.cloned.1.call-done = f32[384,704]{0,1:T(8,128)} async-done(((f32[384,1408]{0,1:T(8,128)}), f32[384,704]{0,1:T(8,128)}) %reduce-scatter.2.cloned.1.call-update) | async-done | bytes 1081360 | tf_op jit(solution)/shard_map/reduce_scatter | solution.py:117
  328.9 1.4 broadcast_add_fusion
  330.3 0.4 copy.24
  330.7 1.0 fusion.48
  (34 shorter events, 0.2 us)
Async XLA Ops:
  7.2 59.6 %all-gather.4.cloned.1.call-start = ((), (), s32[]{:S(2)}) async-start(), calls=%async_computation.1 | async-start | bytes 1622016 | tf_op jit(solution)/shard_map/all_gather | solution.py:53
  8.1 8.8 %collective-permute-start = (bf16[3,16,704]{2,1,0:T(8,128)(2,1)S(1)}, bf16[3,16,704]{2,1,0:T(8,128)(2,1)S(1)}, u32[]{:S(2)}, u32[]{:S(2)}) collective-permute-start(bf16[3,16,704]{2,1,0:T(8,128)(2,1)S(1)} %get-tuple-element.77), channel_id=1, source_target_pairs={{0,8},{8,16},{16,24},{1,9},{9,17},{17,25},{2,10},{10,18},{18,26},{... | collective-permute-start | bytes 202760 | tf_op jit(solution)/shard_map/ppermute | solution.py:17
  13.1 6.2 %collective-permute-start.1 = (bf16[3,16,704]{2,1,0:T(8,128)(2,1)S(1)}, bf16[3,16,704]{2,1,0:T(8,128)(2,1)S(1)}, u32[]{:S(2)}, u32[]{:S(2)}) collective-permute-start(bf16[3,16,704]{2,1,0:T(8,128)(2,1)S(1)} %get-tuple-element.76), channel_id=1, source_target_pairs={{8,0},{16,8},{24,16},{9,1},{17,9},{25,17},{10,2},{18,10},{26,18},{... | collective-permute-start | bytes 202760 | tf_op jit(solution)/shard_map/ppermute | solution.py:20
  18.1 7.7 %copy-start = (bf16[24,16,704]{2,1,0:T(8,128)(2,1)S(1)}, bf16[24,16,704]{2,1,0:T(8,128)(2,1)}, u32[]{:S(2)}) copy-start(bf16[24,16,704]{2,1,0:T(8,128)(2,1)} %param.13) | copy-start | bytes 1622020
  18.1 7.7 %copy-start.5 = (f32[704]{0:T(1024)S(1)}, f32[704]{0:T(1024)}, u32[]{:S(2)}) copy-start(f32[704]{0:T(1024)} %param.15) | copy-start | bytes 8452
  19.5 4.0 %collective-permute-start.2 = (bf16[30,3,704]{2,1,0:T(4,128)(2,1)S(1)}, bf16[30,3,704]{2,1,0:T(4,128)(2,1)S(1)}, u32[]{:S(2)}, u32[]{:S(2)}) collective-permute-start(bf16[30,3,704]{2,1,0:T(4,128)(2,1)S(1)} %get-tuple-element.69), channel_id=1, source_target_pairs={{0,2},{2,4},{4,6},{1,3},{3,5},{5,7},{8,10},{10,12},{12,14},{9,11},... | collective-permute-start | bytes 380168 | tf_op jit(solution)/shard_map/ppermute | solution.py:17
  20.8 5.1 %collective-permute-start.3 = (bf16[30,3,704]{2,1,0:T(4,128)(2,1)S(1)}, bf16[30,3,704]{2,1,0:T(4,128)(2,1)S(1)}, u32[]{:S(2)}, u32[]{:S(2)}) collective-permute-start(bf16[30,3,704]{2,1,0:T(4,128)(2,1)S(1)} %get-tuple-element.70), channel_id=1, source_target_pairs={{2,0},{4,2},{6,4},{3,1},{5,3},{7,5},{10,8},{12,10},{14,12},{11,9},... | collective-permute-start | bytes 380168 | tf_op jit(solution)/shard_map/ppermute | solution.py:20
  40.0 1.1 copy-start.6
  40.0 1.6 copy-start.1
  41.0 49.5 %all-gather.8.cloned.1.call-start = ((), (), s32[]{:S(2)}) async-start(), calls=%async_computation.4 | async-start | bytes 1622016 | tf_op jit(solution)/shard_map/all_gather | solution.py:53
  42.7 122.1 %all-gather.6.cloned.1.call-start = ((), (), s32[]{:S(2)}) async-start(), calls=%async_computation.2 | async-start | bytes 8425472 | tf_op jit(solution)/shard_map/all_gather | solution.py:115
  43.4 250.7 %all-reduce.3.cloned.1.call-start = ((), (), s32[]{:S(2)}) async-start(), calls=%async_computation.5 | async-start | bytes 4325376 | tf_op jit(solution)/shard_map/psum | solution.py:140
  68.5 0.7 copy-start.3
  68.5 0.7 copy-start.7
  68.5 0.7 copy-start.9
  77.8 97.2 %copy-start.2 = (f32[2816]{0:T(1024)S(1)}, f32[2816]{0:T(1024)}, u32[]{:S(2)}) copy-start(f32[2816]{0:T(1024)} %param.20) | copy-start | bytes 33796
  229.1 0.7 copy-start.8
  229.1 99.8 %reduce-scatter.2.cloned.1.call-start = ((), (), s32[]{:S(2)}) async-start(), calls=%async_computation.3 | async-start | bytes 3244032 | tf_op jit(solution)/shard_map/reduce_scatter | solution.py:117
  297.4 5.4 %collective-permute-start.4 = (bf16[3,16,704]{2,1,0:T(8,128)(2,1)S(1)}, bf16[3,16,704]{2,1,0:T(8,128)(2,1)S(1)}, u32[]{:S(2)}, u32[]{:S(2)}) collective-permute-start(bf16[3,16,704]{2,1,0:T(8,128)(2,1)S(1)} %bitcast.23), channel_id=1, source_target_pairs={{0,8},{8,16},{16,24},{1,9},{9,17},{17,25},{2,10},{10,18},{18,26},{... | collective-permute-start | bytes 202760 | tf_op jit(solution)/shard_map/ppermute | solution.py:17
  300.8 6.2 %collective-permute-start.5 = (bf16[3,16,704]{2,1,0:T(8,128)(2,1)S(1)}, bf16[3,16,704]{2,1,0:T(8,128)(2,1)S(1)}, u32[]{:S(2)}, u32[]{:S(2)}) collective-permute-start(bf16[3,16,704]{2,1,0:T(8,128)(2,1)S(1)} %bitcast.22), channel_id=1, source_target_pairs={{8,0},{16,8},{24,16},{9,1},{17,9},{25,17},{10,2},{18,10},{26,18},{... | collective-permute-start | bytes 202760 | tf_op jit(solution)/shard_map/ppermute | solution.py:20
  307.2 4.7 %collective-permute-start.6 = (bf16[30,3,704]{2,1,0:T(4,128)(2,1)S(1)}, bf16[30,3,704]{2,1,0:T(4,128)(2,1)S(1)}, u32[]{:S(2)}, u32[]{:S(2)}) collective-permute-start(bf16[30,3,704]{2,1,0:T(4,128)(2,1)S(1)} %get-tuple-element.67), channel_id=1, source_target_pairs={{2,0},{4,2},{6,4},{3,1},{5,3},{7,5},{10,8},{12,10},{14,12},{11,9},... | collective-permute-start | bytes 380168 | tf_op jit(solution)/shard_map/ppermute | solution.py:20
  308.5 4.1 %collective-permute-start.7 = (bf16[30,3,704]{2,1,0:T(4,128)(2,1)S(1)}, bf16[30,3,704]{2,1,0:T(4,128)(2,1)S(1)}, u32[]{:S(2)}, u32[]{:S(2)}) collective-permute-start(bf16[30,3,704]{2,1,0:T(4,128)(2,1)S(1)} %get-tuple-element.68), channel_id=1, source_target_pairs={{0,2},{2,4},{4,6},{1,3},{3,5},{5,7},{8,10},{10,12},{12,14},{9,11},... | collective-permute-start | bytes 380168 | tf_op jit(solution)/shard_map/ppermute | solution.py:17
  313.1 15.8 %copy-start.4 = (f32[704]{0:T(1024)S(1)}, f32[704]{0:T(1024)}, u32[]{:S(2)}) copy-start(f32[704]{0:T(1024)} %param.23) | copy-start | bytes 8452
Sparse Core Ops, SparseCore 0:
  41.2 25.5 all-gather.3
  68.9 21.6 all-gather.7
  92.8 71.9 all-gather.5
  229.2 64.8 all-reduce.2
  296.3 32.5 reduce-scatter.1
where the time goes:
time: 339 us; the launch traced here: 338 us
  waiting for transfers between devices  180 us (53%)
  matrix products  40.4 us (12%)
  blocking collectives  39.6 us (12%)
  other arithmetic  33.2 us (10%)
  starting transfers between devices  18.3 us (5%)
  between operations  15.4 us (5%)
  local copies, waits for them, and re-layouts  11 us (3%)
    all_gather x1, waiting for transfers between devices, shards(): down_whole = lax.all_gather(down_weight, ('sy', 'sx'), axis=1, tiled=True)  74.2 us
    psum x1, waiting for transfers between devices, shards(): normed_grad = lax.psum(grad_terms, 'tp')  54.7 us
    psum x1, blocking collectives, global_vector(): return lax.psum(placed, ('sy', 'sx', 'tp'))  39.6 us
    all_gather x2, waiting for transfers between devices, all_channels(): return lax.all_gather(rows_array, 'tp', axis=1, tiled=True)  36 us
    convert_element_type x1, other arithmetic, shards(): convolved = (depthwise(extend(features), depth_kernel, image_rows, image_...  14.1 us
    ppermute x4, starting transfers between devices, extended(): lax.ppermute(lax.slice_in_dim(block, block.shape[dim] - width, None, axis...  12.9 us
    dot_general x1, matrix products, shards(): lax.dot_general(preact_grad, up_weight, contract_last, preferred_element_...  12.4 us
    convert_element_type x1, other arithmetic, shards(): feature_grad = (cotangent.astype(jnp.float32) + depthwise(extend(grad_ima...  10.3 us
  transfers between devices with their start and end apart: 13, of which 10 were waited for; matrix products, arithmetic and copies ran while one was open for 12% of the time, Pallas kernels for 0%

commit v1 on v0

--- a/solution.py
+++ b/solution.py
@@ -60,7 +60,7 @@
         local_part,
         (lax.axis_index("tp") * hidden_local,),
     )
-    return lax.psum(placed, ("sy", "sx", "tp"))
+    return lax.psum(lax.psum(placed, "sy"), ("sx", "tp"))
 
 
 def shards(

time: 339 us -> 338 us (level)
  waiting for transfers between devices: 180 us -> 176 us
    psum x1, waiting for transfers between devices: 54.7 us -> 50.3 us  [shards(): normed_grad = lax.psum(grad_terms, 'tp')]
    psum x1 -> x2, blocking collectives: 39.6 us -> 42.3 us  [global_vector(): return lax.psum(lax.psum(placed, 'sy'), ('sx', 'tp'))]
  transfers between devices with their start and end apart: 13 -> 13, of which waited for: 10 -> 10; matrix products, arithmetic and copies ran while one was open for 12% -> 13% of each run, Pallas kernels for 0% -> 0%
where the time goes in v1:
time: 338 us; the launch traced here: 337 us
  waiting for transfers between devices  176 us (52%)
  blocking collectives  42.3 us (13%)
  matrix products  41.2 us (12%)
  other arithmetic  33.2 us (10%)
  starting transfers between devices  18 us (5%)
  between operations  15.4 us (5%)
  local copies, waits for them, and re-layouts  11.1 us (3%)
    all_gather x1, waiting for transfers between devices, shards(): down_whole = lax.all_gather(down_weight, ('sy', 'sx'), axis=1, tiled=True)  74.2 us
    psum x1, waiting for transfers between devices, shards(): normed_grad = lax.psum(grad_terms, 'tp')  50.3 us
    psum x2, blocking collectives, global_vector(): return lax.psum(lax.psum(placed, 'sy'), ('sx', 'tp'))  42.3 us
    all_gather x2, waiting for transfers between devices, all_channels(): return lax.all_gather(rows_array, 'tp', axis=1, tiled=True)  36 us
    convert_element_type x1, other arithmetic, shards(): convolved = (depthwise(extend(features), depth_kernel, image_rows, image_...  14.1 us
    ppermute x4, starting transfers between devices, extended(): lax.ppermute(lax.slice_in_dim(block, block.shape[dim] - width, None, axis...  12.7 us
    dot_general x1, matrix products, shards(): lax.dot_general(preact_grad, up_weight, contract_last, preferred_element_...  12.4 us
    convert_element_type x1, other arithmetic, shards(): feature_grad = (cotangent.astype(jnp.float32) + depthwise(extend(grad_ima...  10.3 us
  transfers between devices with their start and end apart: 13, of which 10 were waited for; matrix products, arithmetic and copies ran while one was open for 13% of the time, Pallas kernels for 0%

profile of v1, /device:TPU:0, one launch (start us, length us, event | category | flops | bytes accessed | tf_op | source)
XLA Modules:
  0.0 337.4 jit_solution(18162666066133131755)
XLA Ops:
  7.2 0.0 all-gather.4.cloned.1.call-start
  7.2 0.9 fusion.105
  8.1 4.9 %collective-permute-start = (bf16[3,16,704]{2,1,0:T(8,128)(2,1)S(1)}, bf16[3,16,704]{2,1,0:T(8,128)(2,1)S(1)}, u32[]{:S(2)}, u32[]{:S(2)}) collective-permute-start(bf16[3,16,704]{2,1,0:T(8,128)(2,1)S(1)} %get-tuple-element.79), channel_id=1, source_target_pairs={{0,8},{8,16},{16,24},{1,9},{9,17},{17,25},{2,10},{10,18},{18,26},{... | collective-permute-start | bytes 202760 | tf_op jit(solution)/shard_map/ppermute | solution.py:17
  13.1 1.3 collective-permute-start.1
  14.4 1.4 slice_reduce_fusion.48
  15.8 1.1 slice_reduce_fusion.46
  16.9 1.2 constant_dynamic-update-slice_fusion.3
  18.2 1.2 collective-permute-done.1
  19.3 0.1 fusion.103
  19.5 1.3 collective-permute-start.2
  20.8 1.3 collective-permute-start.3
  22.1 1.4 slice_reduce_fusion.47
  23.5 2.4 collective-permute-done.3
  25.9 14.1 %add_convert_fusion.2 = bf16[24,16,704]{2,1,0:T(8,128)(2,1)S(1)} fusion(bf16[24,16,704]{2,1,0:T(8,128)(2,1)S(1)} %copy-done, bf16[30,16,704]{2,1,0:T(8,128)(2,1)S(1)} %get-tuple-element.83, bf16[30,3,704]{2,1,0:T(4,128)(2,1)S(1)} %collective-permute-done.3, bf16[30,3,704]{2,1,0:T(4,128)(2,1)S(1)} %collective-permute-done.2, ...), kind=kLoop, calls=%fused_computation.149 | loop fusion | flops 74072064 | bytes 5395456 | tf_op jit(solution)/shard_map/convert_element_type | solution.py:96
  40.0 1.0 copy.21
  41.0 0.0 all-gather.4.cloned.1.call-update
  41.0 0.0 all-gather.8.cloned.1.call-start
  41.1 0.1 broadcast_in_dim.4
  41.2 0.1 convert_element_type.364
  41.3 0.1 copy.26
  41.4 0.1 broadcast_in_dim.5.clone
  41.4 0.1 convert_element_type.419
  41.6 0.2 copy.25
  41.8 0.9 multiply_convert_fusion.1
  42.7 0.0 all-gather.8.cloned.1.call-update
  42.7 0.0 all-gather.6.cloned.1.call-start
  42.7 0.7 all-gather.6.cloned.1.call-update
  43.4 0.0 all-reduce.4.cloned.1.call-start
  43.5 23.3 %all-gather.4.cloned.1.call-done = bf16[384,1408]{0,1:T(8,128)(2,1)} async-done(((bf16[384,704]{0,1:T(8,128)(2,1)}), bf16[384,1408]{0,1:T(8,128)(2,1)}) %all-gather.4.cloned.1.call-update) | async-done | bytes 1081360 | tf_op jit(solution)/shard_map/all_gather | solution.py:53
  66.7 1.7 copy.22
  68.5 0.2 convert_reduce_fusion
  68.7 0.4 fusion.15
  69.2 8.6 %convolution_add_fusion = f32[384,2816]{1,0:T(8,128)} fusion(bf16[1408,2816]{1,0:T(8,128)(2,1)} %param.18, f32[2816]{0:T(1024)S(1)} %copy-done.7, f32[1408]{0:T(1024)S(1)} %copy-done.9, f32[1408]{0:T(1024)S(1)} %copy-done.3, bf16[384,1408]{1,0:T(8,128)(2,1)S(1)} %copy.22, f32[384]{0:T(512)S(1)} %add_rsqrt_fusion, f32[384]{0:T(512)S(1)} %broadcast_multiply_fusion.3), kind=kOutput, calls=%fused_computation.62 | convolution fusion | flops 3049390080 | bytes 13362176 | tf_op jit(solution)/shard_map/dot_general | solution.py:103
  77.8 12.8 %all-gather.8.cloned.1.call-done = bf16[384,1408]{0,1:T(8,128)(2,1)} async-done(((bf16[384,704]{0,1:T(8,128)(2,1)}), bf16[384,1408]{0,1:T(8,128)(2,1)}) %all-gather.8.cloned.1.call-update) | async-done | bytes 1081360 | tf_op jit(solution)/shard_map/all_gather | solution.py:53
  90.6 74.2 %all-gather.6.cloned.1.call-done = bf16[2816,1408]{0,1:T(8,128)(2,1)} async-done(((bf16[2816,88]{0,1:T(8,128)(2,1)}), bf16[2816,1408]{0,1:T(8,128)(2,1)}) %all-gather.6.cloned.1.call-update) | async-done | bytes 7929872 | tf_op jit(solution)/shard_map/all_gather | solution.py:115
  164.8 9.9 %fusion.10 = (f32[2816]{0:T(1024)S(1)}, f32[2816]{0:T(1024)S(1)}, bf16[384,2816]{1,0:T(8,128)(2,1)}, f32[384,2816]{1,0:T(8,128)}) fusion(f32[384]{0:T(512)S(1)} %convert_element_type.419, f32[384,2816]{1,0:T(8,128)} %convolution_add_fusion, bf16[384,1408]{0,1:T(8,128)(2,1)} %all-gather.8.cloned.1.call-done, bf16[2816,1408]{0,1:T(8,128)(2,1)} %all-gather.6.cloned.1.call-done), kind=kOutput, calls=%fused_computation.57 | convolution fusion | flops 3056953856 | bytes 19848704 | tf_op jit(solution)/shard_map/dot_general | solution.py:124
  174.7 0.3 dynamic_update_slice.6
  175.0 0.1 multiply_dynamic-update-slice_fusion
  175.2 17.8 %all-reduce.1 = (f32[5632]{0:T(1024)S(1)}, f32[5632]{0:T(1024)S(1)}) all-reduce(f32[5632]{0:T(1024)S(1)} %dynamic_update_slice.6, f32[5632]{0:T(1024)S(1)} %multiply_dynamic-update-slice_fusion), channel_id=1, replica_groups=mesh['sy'=4,'sx'=4,'tp'=2] {'sy'}, use_global_device_ids=true, to_apply=%region_3.0 | all-reduce | flops 11264 | bytes 90112 | tf_op jit(solution)/shard_map/psum | solution.py:63
  192.9 24.5 %all-reduce = (f32[5632]{0:T(1024)S(1)}, f32[5632]{0:T(1024)S(1)}) all-reduce(f32[5632]{0:T(1024)S(1)} %get-tuple-element.59, f32[5632]{0:T(1024)S(1)} %get-tuple-element.60), channel_id=1, replica_groups=mesh['sy'=4,'sx'=4,'tp'=2] {'sx','tp'}, use_global_device_ids=true, to_apply=%region_4.0 | all-reduce | flops 11264 | bytes 90112 | tf_op jit(solution)/shard_map/psum | solution.py:63
  217.5 0.6 multiply_reduce_fusion.1
  219.4 0.1 multiply_add_fusion
  219.5 12.4 %fusion.21 = f32[384,1408]{1,0:T(8,128)} fusion(bf16[1408,2816]{1,0:T(8,128)(2,1)} %param.18, f32[384,2816]{1,0:T(8,128)} %convolution_add_fusion, bf16[384,2816]{1,0:T(8,128)(2,1)} %get-tuple-element.65, f32[384,2816]{1,0:T(8,128)} %get-tuple-element.85, f32[2816]{0:T(1024)S(1)} %get-tuple-element.64, f32[2816]{0:T(1024)S(1)} %get-tuple-element.86, ...), kind=kOutput, calls=%fused_computation.74 | convolution fusion | flops 3062366208 | bytes 20941312 | tf_op jit(solution)/shard_map/dot_general | solution.py:137
  231.9 0.0 reduce-scatter.2.cloned.1.call-start
  231.9 0.6 copy-done.8
  232.6 10.3 %fusion.16 = f32[384,1408]{0,1:T(8,128)} fusion(bf16[2816,1408]{0,1:T(8,128)(2,1)} %all-gather.6.cloned.1.call-done, bf16[384,2816]{1,0:T(8,128)(2,1)} %get-tuple-element.65, f32[2816]{0:T(1024)S(1)} %copy-done.8, f32[2816]{0:T(1024)S(1)} %get-tuple-element.63, f32[2816]{0:T(1024)S(1)} %copy-done.2), kind=kOutput, calls=%fused_computation.68 | convolution fusion | flops 3051552768 | bytes 12289024 | tf_op jit(solution)/shard_map/dot_general | solution.py:116
  242.9 50.3 %all-reduce.4.cloned.1.call-done = f32[384,1408]{1,0:T(8,128)} async-done(((f32[384,1408]{1,0:T(8,128)}), f32[384,1408]{1,0:T(8,128)}) %all-reduce.4.cloned.1.call-update) | async-done | bytes 2162704 | tf_op jit(solution)/shard_map/psum | solution.py:140
  293.2 2.2 fusion.102
  295.5 1.0 fusion.51
  296.5 3.4 %collective-permute-start.4 = (bf16[3,16,704]{2,1,0:T(8,128)(2,1)S(1)}, bf16[3,16,704]{2,1,0:T(8,128)(2,1)S(1)}, u32[]{:S(2)}, u32[]{:S(2)}) collective-permute-start(bf16[3,16,704]{2,1,0:T(8,128)(2,1)S(1)} %bitcast.23), channel_id=1, source_target_pairs={{0,8},{8,16},{16,24},{1,9},{9,17},{17,25},{2,10},{10,18},{18,26},{... | collective-permute-start | bytes 202760 | tf_op jit(solution)/shard_map/ppermute | solution.py:17
  299.9 1.3 collective-permute-start.5
  301.2 0.7 collective-permute-done.4
  301.8 4.3 %collective-permute-done.5 = bf16[3,16,704]{2,1,0:T(8,128)(2,1)S(1)} collective-permute-done((bf16[3,16,704]{2,1,0:T(8,128)(2,1)S(1)}, bf16[3,16,704]{2,1,0:T(8,128)(2,1)S(1)}, u32[]{:S(2)}, u32[]{:S(2)}) %collective-permute-start.5) | collective-permute-done | bytes 67616 | tf_op jit(solution)/shard_map/ppermute | solution.py:20
  306.1 0.2 pad_maximum_fusion.7
  306.3 1.3 collective-permute-start.6
  307.6 3.0 collective-permute-start.7
  310.7 0.1 copy.20
  310.7 0.9 collective-permute-done.7
  311.7 0.6 pad_maximum_fusion
  312.2 10.3 %add_convert_fusion.1 = bf16[24,16,704]{2,1,0:T(8,128)(2,1)} fusion(bf16[24,16,704]{2,1,0:T(8,128)(2,1)S(1)} %bitcast.18, bf16[3,16,704]{2,1,0:T(8,128)(2,1)S(1)} %collective-permute-done.4, bf16[3,16,704]{2,1,0:T(8,128)(2,1)S(1)} %collective-permute-done.5, bf16[30,19,704]{2,1,0:T(8,128)(2,1)S(1)} %get-tuple-element.68, ...), kind=kLoop, calls=%fused_computation.148 | loop fusion | flops 41902080 | bytes 24603392 | tf_op jit(solution)/shard_map/convert_element_type | solution.py:153
  322.6 5.4 %reduce-scatter.2.cloned.1.call-done = f32[384,704]{0,1:T(8,128)} async-done(((f32[384,1408]{0,1:T(8,128)}), f32[384,704]{0,1:T(8,128)}) %reduce-scatter.2.cloned.1.call-update) | async-done | bytes 1081360 | tf_op jit(solution)/shard_map/reduce_scatter | solution.py:117
  328.0 1.4 broadcast_add_fusion
  329.4 0.4 copy.24
  329.8 1.0 fusion.48
  (35 shorter events, 0.2 us)
Async XLA Ops:
  7.2 59.6 %all-gather.4.cloned.1.call-start = ((), (), s32[]{:S(2)}) async-start(), calls=%async_computation.1 | async-start | bytes 1622016 | tf_op jit(solution)/shard_map/all_gather | solution.py:53
  8.1 8.8 %collective-permute-start = (bf16[3,16,704]{2,1,0:T(8,128)(2,1)S(1)}, bf16[3,16,704]{2,1,0:T(8,128)(2,1)S(1)}, u32[]{:S(2)}, u32[]{:S(2)}) collective-permute-start(bf16[3,16,704]{2,1,0:T(8,128)(2,1)S(1)} %get-tuple-element.79), channel_id=1, source_target_pairs={{0,8},{8,16},{16,24},{1,9},{9,17},{17,25},{2,10},{10,18},{18,26},{... | collective-permute-start | bytes 202760 | tf_op jit(solution)/shard_map/ppermute | solution.py:17
  13.1 6.2 %collective-permute-start.1 = (bf16[3,16,704]{2,1,0:T(8,128)(2,1)S(1)}, bf16[3,16,704]{2,1,0:T(8,128)(2,1)S(1)}, u32[]{:S(2)}, u32[]{:S(2)}) collective-permute-start(bf16[3,16,704]{2,1,0:T(8,128)(2,1)S(1)} %get-tuple-element.78), channel_id=1, source_target_pairs={{8,0},{16,8},{24,16},{9,1},{17,9},{25,17},{10,2},{18,10},{26,18},{... | collective-permute-start | bytes 202760 | tf_op jit(solution)/shard_map/ppermute | solution.py:20
  18.1 7.7 %copy-start = (bf16[24,16,704]{2,1,0:T(8,128)(2,1)S(1)}, bf16[24,16,704]{2,1,0:T(8,128)(2,1)}, u32[]{:S(2)}) copy-start(bf16[24,16,704]{2,1,0:T(8,128)(2,1)} %param.13) | copy-start | bytes 1622020
  18.1 7.7 %copy-start.5 = (f32[704]{0:T(1024)S(1)}, f32[704]{0:T(1024)}, u32[]{:S(2)}) copy-start(f32[704]{0:T(1024)} %param.15) | copy-start | bytes 8452
  19.5 4.0 %collective-permute-start.2 = (bf16[30,3,704]{2,1,0:T(4,128)(2,1)S(1)}, bf16[30,3,704]{2,1,0:T(4,128)(2,1)S(1)}, u32[]{:S(2)}, u32[]{:S(2)}) collective-permute-start(bf16[30,3,704]{2,1,0:T(4,128)(2,1)S(1)} %get-tuple-element.71), channel_id=1, source_target_pairs={{0,2},{2,4},{4,6},{1,3},{3,5},{5,7},{8,10},{10,12},{12,14},{9,11},... | collective-permute-start | bytes 380168 | tf_op jit(solution)/shard_map/ppermute | solution.py:17
  20.8 5.1 %collective-permute-start.3 = (bf16[30,3,704]{2,1,0:T(4,128)(2,1)S(1)}, bf16[30,3,704]{2,1,0:T(4,128)(2,1)S(1)}, u32[]{:S(2)}, u32[]{:S(2)}) collective-permute-start(bf16[30,3,704]{2,1,0:T(4,128)(2,1)S(1)} %get-tuple-element.72), channel_id=1, source_target_pairs={{2,0},{4,2},{6,4},{3,1},{5,3},{7,5},{10,8},{12,10},{14,12},{11,9},... | collective-permute-start | bytes 380168 | tf_op jit(solution)/shard_map/ppermute | solution.py:20
  40.0 1.1 copy-start.6
  40.0 1.6 copy-start.1
  41.0 49.5 %all-gather.8.cloned.1.call-start = ((), (), s32[]{:S(2)}) async-start(), calls=%async_computation.4 | async-start | bytes 1622016 | tf_op jit(solution)/shard_map/all_gather | solution.py:53
  42.7 122.1 %all-gather.6.cloned.1.call-start = ((), (), s32[]{:S(2)}) async-start(), calls=%async_computation.2 | async-start | bytes 8425472 | tf_op jit(solution)/shard_map/all_gather | solution.py:115
  43.4 249.8 %all-reduce.4.cloned.1.call-start = ((), (), s32[]{:S(2)}) async-start(), calls=%async_computation.5 | async-start | bytes 4325376 | tf_op jit(solution)/shard_map/psum | solution.py:140
  68.5 0.7 copy-start.3
  68.5 0.7 copy-start.7
  68.5 0.7 copy-start.9
  77.8 97.2 %copy-start.2 = (f32[2816]{0:T(1024)S(1)}, f32[2816]{0:T(1024)}, u32[]{:S(2)}) copy-start(f32[2816]{0:T(1024)} %param.20) | copy-start | bytes 33796
  231.9 0.7 copy-start.8
  231.9 96.1 %reduce-scatter.2.cloned.1.call-start = ((), (), s32[]{:S(2)}) async-start(), calls=%async_computation.3 | async-start | bytes 3244032 | tf_op jit(solution)/shard_map/reduce_scatter | solution.py:117
  296.5 5.4 %collective-permute-start.4 = (bf16[3,16,704]{2,1,0:T(8,128)(2,1)S(1)}, bf16[3,16,704]{2,1,0:T(8,128)(2,1)S(1)}, u32[]{:S(2)}, u32[]{:S(2)}) collective-permute-start(bf16[3,16,704]{2,1,0:T(8,128)(2,1)S(1)} %bitcast.23), channel_id=1, source_target_pairs={{0,8},{8,16},{16,24},{1,9},{9,17},{17,25},{2,10},{10,18},{18,26},{... | collective-permute-start | bytes 202760 | tf_op jit(solution)/shard_map/ppermute | solution.py:17
  299.9 6.2 %collective-permute-start.5 = (bf16[3,16,704]{2,1,0:T(8,128)(2,1)S(1)}, bf16[3,16,704]{2,1,0:T(8,128)(2,1)S(1)}, u32[]{:S(2)}, u32[]{:S(2)}) collective-permute-start(bf16[3,16,704]{2,1,0:T(8,128)(2,1)S(1)} %bitcast.22), channel_id=1, source_target_pairs={{8,0},{16,8},{24,16},{9,1},{17,9},{25,17},{10,2},{18,10},{26,18},{... | collective-permute-start | bytes 202760 | tf_op jit(solution)/shard_map/ppermute | solution.py:20
  306.3 4.4 %collective-permute-start.6 = (bf16[30,3,704]{2,1,0:T(4,128)(2,1)S(1)}, bf16[30,3,704]{2,1,0:T(4,128)(2,1)S(1)}, u32[]{:S(2)}, u32[]{:S(2)}) collective-permute-start(bf16[30,3,704]{2,1,0:T(4,128)(2,1)S(1)} %get-tuple-element.69), channel_id=1, source_target_pairs={{2,0},{4,2},{6,4},{3,1},{5,3},{7,5},{10,8},{12,10},{14,12},{11,9},... | collective-permute-start | bytes 380168 | tf_op jit(solution)/shard_map/ppermute | solution.py:20
  307.6 4.1 %collective-permute-start.7 = (bf16[30,3,704]{2,1,0:T(4,128)(2,1)S(1)}, bf16[30,3,704]{2,1,0:T(4,128)(2,1)S(1)}, u32[]{:S(2)}, u32[]{:S(2)}) collective-permute-start(bf16[30,3,704]{2,1,0:T(4,128)(2,1)S(1)} %get-tuple-element.70), channel_id=1, source_target_pairs={{0,2},{2,4},{4,6},{1,3},{3,5},{5,7},{8,10},{10,12},{12,14},{9,11},... | collective-permute-start | bytes 380168 | tf_op jit(solution)/shard_map/ppermute | solution.py:17
  312.2 15.8 %copy-start.4 = (f32[704]{0:T(1024)S(1)}, f32[704]{0:T(1024)}, u32[]{:S(2)}) copy-start(f32[704]{0:T(1024)} %param.23) | copy-start | bytes 8452
Sparse Core Ops, SparseCore 0:
  41.2 25.5 all-gather.3
  68.9 21.6 all-gather.7
  92.8 71.9 all-gather.5
  232.0 61.1 all-reduce.3
  295.4 32.5 reduce-scatter.1
